TPU v7x, 32 devices: a whole 2x2x4 slice. The times are simulated.
32 devices in a mesh: wide: 16 (over z, y, core), narrow: 2 (over x).
Axes of the slice: x: 2, y: 2, z: 4, core: 2. Of those that a mesh axis runs over, the one named last changes fastest.
Arguments:
- vol_points: float32 [3, 32768], P(None, 'wide'), may hold values from 0 to 1
- vol_adjoint: bfloat16 [48, 32768], P(None, 'wide'), may hold values from -6 to 6
- surf_points: float32 [3, 4096], P(None, ('narrow', 'wide')), may hold values from 0 to 1
- tile_mask: int32 [256, 32], P('wide', 'narrow'), may hold values 0 or 1
Outputs:
- solution: float32 [48, 4096], P(None, ('narrow', 'wide'))
- residual: float32 [48, 4096], P(None, ('narrow', 'wide'))
All inputs are finite; a program needn't handle non-finite values. No bound on the sum of `tile_mask` on one device may be relied on, other than what follows from the above.
Results may differ from a plain program's by a relative error of at most 0.0039.
Values sent between devices are 32-bit elements; how exact they have to be, the bound alone decides.
A program may use at most 64 MiB of HBM per device.

v0:
```python
import math

import jax
import jax.numpy as jnp
from jax import lax
from jax.sharding import PartitionSpec as P

TILE = 128


RADIUS = 0.15
KERNEL_GAIN = 3200.0
RHS_GAIN = 28.0
LOWER_EDGE = 1.0
UPPER_EDGE = 4.0


def kernel_block(sources, targets):
    squared = jnp.zeros((sources.shape[1], targets.shape[1]), jnp.float32)
    for component in range(3):
        offset = sources[component][:, None] - targets[component][None, :]
        squared = squared + offset * offset
    scaled = jnp.sqrt(squared) / RADIUS
    remain = jnp.maximum(1.0 - scaled, 0.0)
    return remain**4 * (4.0 * scaled + 1.0)


def apply_operator(field, columns, row_coords, total_surface):
    empty = jnp.zeros((field.shape[0], row_coords.shape[1]), jnp.float32)
    piece = lax.all_gather(field, "wide", axis=1, tiled=True)
    count = piece.shape[1]
    stride = math.gcd(count, 256)

    def one_block(index, accum):
        offset = index * stride
        block_vals = lax.dynamic_slice_in_dim(piece, offset, stride, 1)
        sources = lax.dynamic_slice_in_dim(columns, offset, stride, 1)
        values = kernel_block(sources, row_coords)
        return accum + jnp.dot(
            block_vals, values, precision=lax.Precision.HIGHEST, preferred_element_type=jnp.float32
        )

    partial_rows = lax.fori_loop(0, count // stride, one_block, empty)
    mixed = lax.psum_scatter(partial_rows, "narrow", scatter_dimension=1, tiled=True)
    return field + KERNEL_GAIN / total_surface * mixed


def body(vol_points, vol_adjoint, surf_points, tile_mask):
    columns = lax.all_gather(surf_points, "wide", axis=1, tiled=True)
    row_coords = lax.all_gather(surf_points, "narrow", axis=1, tiled=True)
    span = columns.shape[1]
    volume_rows = vol_points.shape[1]
    adjoint_cols = vol_adjoint.shape[0]
    width = math.gcd(span, 256)
    total_volume = volume_rows * lax.axis_size("wide")
    total_surface = surf_points.shape[1] * lax.axis_size("wide") * lax.axis_size("narrow")

    def surface_block(index, total):
        start = index * width
        targets = lax.dynamic_slice_in_dim(columns, start, width, 1)
        mask_cols = lax.dynamic_slice_in_dim(tile_mask, start // TILE, width // TILE, 1)
        expanded = jnp.broadcast_to(
            mask_cols[:, None, :, None], (volume_rows // TILE, TILE, width // TILE, TILE)
        )
        expanded = expanded.reshape(volume_rows, width).astype(jnp.float32)
        values = (kernel_block(vol_points, targets) * expanded).astype(jnp.bfloat16)
        part = jnp.dot(vol_adjoint, values, preferred_element_type=jnp.float32)
        return lax.dynamic_update_slice_in_dim(total, part, start, 1)

    term = lax.fori_loop(
        0, span // width, surface_block, jnp.zeros((adjoint_cols, span), jnp.float32)
    )
    rhs = lax.psum_scatter(term, "wide", scatter_dimension=1, tiled=True) * (
        RHS_GAIN / math.sqrt(total_volume)
    )
    centre = (LOWER_EDGE + UPPER_EDGE) / 2.0
    half_width = (UPPER_EDGE - LOWER_EDGE) / 2.0
    sigma = centre / half_width
    rho_zero = 1.0 / sigma
    rho_one = 1.0 / (2.0 * sigma - rho_zero)
    first = rhs / centre
    near = rhs - apply_operator(first, columns, row_coords, total_surface)
    update = rho_one * rho_zero * first + 2.0 * rho_one / half_width * near
    solution = first + update
    residual = near - apply_operator(update, columns, row_coords, total_surface)
    return (solution, residual)


def solution(mesh):
    return jax.shard_map(
        body,
        mesh=mesh,
        in_specs=(
            P(None, "wide"),
            P(None, "wide"),
            P(None, ("narrow", "wide")),
            P("wide", "narrow"),
        ),
        out_specs=(P(None, ("narrow", "wide")), P(None, ("narrow", "wide"))),
        check_vma=False,
    )
```

profile of v0, /device:TPU:0, one launch (start us, length us, event | category | flops | bytes accessed | tf_op | source)
XLA Modules:
  0.0 188.5 jit_solution(5529605285063595386)
XLA Ops:
  7.2 23.4 %all_gather.12 = f32[3,2048]{1,0:T(4,128)S(1)} all-gather(f32[3,128]{1,0:T(4,128)} %param.12), channel_id=1, replica_groups=mesh['wide'=16,'narrow'=2] {'wide'}, dimensions={1}, use_global_device_ids=true | all-gather | bytes 26112 | tf_op jit(solution)/shard_map/all_gather | solution.py:49
  30.7 28.1 %while.47 = (s32[]{:T(128)}, f32[48,2048]{1,0:T(8,128)S(1)}, f32[3,2048]{1,0:T(4,128)}, f32[3,2048]{1,0:T(4,128)S(1)}, s32[16,16]{1,0:T(8,128)}, /*index=5*/bf16...) while((s32[]{:T(128)}, f32[48,2048]{1,0:T(8,128)S(1)}, ...), condition=%wide.region_1.2_spmd, body=%wide.region_0.1_spmd.sunk | while | flops 59768888 | bytes 5408598 | solution.py:70
  30.7 0.8 dynamic-slice_convert_fusion.2
  31.6 0.6 broadcast_in_dim.24
  32.3 1.9 fusion.89
  34.2 0.8 dynamic-slice_convert_fusion.2
  35.1 0.6 broadcast_in_dim.24
  35.8 1.9 fusion.89
  37.8 0.8 dynamic-slice_convert_fusion.2
  38.6 0.6 broadcast_in_dim.24
  39.3 1.9 fusion.89
  41.3 0.8 dynamic-slice_convert_fusion.2
  42.1 0.6 broadcast_in_dim.24
  42.8 1.9 fusion.89
  44.8 0.8 dynamic-slice_convert_fusion.2
  45.6 0.6 broadcast_in_dim.24
  46.4 1.9 fusion.89
  48.3 0.8 dynamic-slice_convert_fusion.2
  49.1 0.6 broadcast_in_dim.24
  49.9 1.9 fusion.89
  51.8 0.8 dynamic-slice_convert_fusion.2
  52.6 0.6 broadcast_in_dim.24
  53.4 1.9 fusion.89
  55.3 0.8 dynamic-slice_convert_fusion.2
  56.1 0.6 broadcast_in_dim.24
  56.9 1.9 fusion.89
  58.8 0.7 copy-done
  59.6 4.3 %all_gather.14 = f32[3,256]{1,0:T(4,128)S(1)} all-gather(f32[3,128]{1,0:T(4,128)S(1)} %copy-done.6), channel_id=1, replica_groups=mesh['wide'=16,'narrow'=2] {'narrow'}, dimensions={1}, use_global_device_ids=true | all-gather | bytes 4608 | tf_op jit(solution)/shard_map/all_gather | solution.py:50
  64.0 47.3 %reduce-scatter.4.cloned.1.call-done = f32[48,128]{1,0:T(8,128)} async-done(((f32[48,2048]{1,0:T(8,128)}), f32[48,128]{1,0:T(8,128)}) %reduce-scatter.4.cloned.1.call-update) | async-done | bytes 24592 | tf_op jit(solution)/shard_map/reduce_scatter | solution.py:73
  111.2 0.7 broadcast_multiply_fusion
  112.0 20.4 %all_gather.13 = f32[48,2048]{1,0:T(8,128)S(1)} all-gather(f32[48,128]{1,0:T(8,128)S(1)} %broadcast_multiply_fusion), channel_id=1, replica_groups=mesh['wide'=16,'narrow'=2] {'wide'}, dimensions={1}, use_global_device_ids=true | all-gather | bytes 417792 | tf_op jit(solution)/shard_map/all_gather | solution.py:30
  132.4 5.0 %while.48 = (s32[]{:T(128)}, f32[48,256]{1,0:T(8,128)S(1)}, f32[48,2048]{1,0:T(8,128)S(1)}, f32[3,2048]{1,0:T(4,128)S(1)}, f32[3,256]{1,0:T(4,128)S(1)}, /*index...) while((s32[]{:T(128)}, f32[48,256]{1,0:T(8,128)S(1)}, ...), condition=%wide.region_4.5_spmd.clone, body=%wide.region_3.4_spmd.clone.sunk | while | flops 38821896 | bytes 166093 | solution.py:43
  132.5 0.5 convolution_add_fusion.4
  133.0 0.1 constant_dynamic-slice_fusion.7
  133.1 0.5 convolution_add_fusion.4
  133.7 0.1 constant_dynamic-slice_fusion.7
  133.8 0.5 convolution_add_fusion.4
  134.3 0.1 constant_dynamic-slice_fusion.7
  134.4 0.5 convolution_add_fusion.4
  134.9 0.1 constant_dynamic-slice_fusion.7
  135.0 0.5 convolution_add_fusion.4
  135.6 0.5 convolution_add_fusion.4
  136.2 0.1 constant_dynamic-slice_fusion.7
  136.3 0.5 convolution_add_fusion.4
  136.8 0.1 constant_dynamic-slice_fusion.7
  136.9 0.5 convolution_add_fusion.4
  137.4 0.6 copy-done.4
  138.1 7.2 %reduce-scatter.6.cloned.1.call-done = f32[48,128]{1,0:T(8,128)} async-done(((f32[48,256]{1,0:T(8,128)}), f32[48,128]{1,0:T(8,128)}) %reduce-scatter.6.cloned.1.call-update) | async-done | bytes 24592 | tf_op jit(solution)/shard_map/reduce_scatter | solution.py:44
  145.3 0.7 multiply_add_fusion
  146.1 22.5 %all_gather.15 = f32[48,2048]{1,0:T(8,128)S(1)} all-gather(f32[48,128]{1,0:T(8,128)S(1)} %multiply_add_fusion), channel_id=1, replica_groups=mesh['wide'=16,'narrow'=2] {'wide'}, dimensions={1}, use_global_device_ids=true | all-gather | bytes 417792 | tf_op jit(solution)/shard_map/all_gather | solution.py:30
  168.6 5.0 %while.49 = (s32[]{:T(128)}, f32[48,256]{1,0:T(8,128)S(1)}, f32[48,2048]{1,0:T(8,128)S(1)}, f32[3,2048]{1,0:T(4,128)S(1)}, f32[3,256]{1,0:T(4,128)S(1)}, /*index...) while((s32[]{:T(128)}, f32[48,256]{1,0:T(8,128)S(1)}, ...), condition=%wide.region_7.8_spmd.clone, body=%wide.region_6.7_spmd.clone.sunk | while | flops 38821896 | bytes 166093 | solution.py:43
  168.7 0.5 convolution_add_fusion.5
  169.2 0.1 constant_dynamic-slice_fusion.8
  169.3 0.5 convolution_add_fusion.5
  169.9 0.5 convolution_add_fusion.5
  170.6 0.5 convolution_add_fusion.5
  171.2 0.5 convolution_add_fusion.5
  171.8 0.5 convolution_add_fusion.5
  172.3 0.1 constant_dynamic-slice_fusion.8
  172.4 0.5 convolution_add_fusion.5
  173.1 0.5 convolution_add_fusion.5
  173.6 0.6 copy-done.5
  174.2 6.3 %reduce-scatter.8.cloned.1.call-done = f32[48,128]{1,0:T(8,128)} async-done(((f32[48,256]{1,0:T(8,128)}), f32[48,128]{1,0:T(8,128)}) %reduce-scatter.8.cloned.1.call-update) | async-done | bytes 24592 | tf_op jit(solution)/shard_map/reduce_scatter | solution.py:44
  180.6 1.4 add_subtract_fusion
  (74 shorter events, 1.8 us)
Async XLA Ops:
  7.2 104.1 %reduce-scatter.4.cloned.1.call-start = ((), (), s32[]{:S(2)}) async-start(), calls=%async_computation.3 | async-start | bytes 417792 | tf_op jit(solution)/shard_map/reduce_scatter | solution.py:73
  30.7 29.0 %copy-start.6 = (f32[3,128]{1,0:T(4,128)S(1)}, f32[3,128]{1,0:T(4,128)}, u32[]{:S(2)}) copy-start(f32[3,128]{1,0:T(4,128)} %param.12) | copy-start | bytes 4612
  30.7 1.6 copy-start.1
  30.7 1.6 copy-start.7
  34.2 1.6 copy-start.1
  34.2 1.6 copy-start.7
  37.7 1.6 copy-start.1
  37.7 1.6 copy-start.7
  41.2 1.6 copy-start.1
  41.2 1.6 copy-start.7
  44.7 1.6 copy-start.1
  44.7 1.6 copy-start.7
  48.2 1.6 copy-start.1
  48.3 1.6 copy-start.7
  51.7 1.6 copy-start.1
  51.8 1.6 copy-start.7
  55.3 1.6 copy-start.1
  55.3 1.6 copy-start.7
  58.8 0.8 copy-start
  59.5 85.8 %reduce-scatter.6.cloned.1.call-start = ((), (), s32[]{:S(2)}) async-start(), calls=%async_computation.4 | async-start | bytes 73728 | tf_op jit(solution)/shard_map/reduce_scatter | solution.py:44
  132.4 12.9 %copy-start.2 = (f32[48,128]{1,0:T(8,128)S(1)}, f32[48,128]{1,0:T(8,128)}, u32[]{:S(2)}) copy-start(f32[48,128]{1,0:T(8,128)} %reduce-scatter.4.cloned.1.call-done) | copy-start | bytes 73732
  137.4 0.6 copy-start.4
  138.0 42.5 %reduce-scatter.8.cloned.1.call-start = ((), (), s32[]{:S(2)}) async-start(), calls=%async_computation.5 | async-start | bytes 73728 | tf_op jit(solution)/shard_map/reduce_scatter | solution.py:44
  168.6 12.0 %copy-start.3 = (f32[48,128]{1,0:T(8,128)S(1)}, f32[48,128]{1,0:T(8,128)}, u32[]{:S(2)}) copy-start(f32[48,128]{1,0:T(8,128)} %reduce-scatter.6.cloned.1.call-done) | copy-start | bytes 73732
  173.6 0.6 copy-start.5
Sparse Core Ops, SparseCore 0:
  59.7 51.5 reduce-scatter.3
  138.2 7.0 reduce-scatter.5
  174.3 6.1 reduce-scatter.7
where the time goes:
time: 189 us; the launch traced here: 188 us
  blocking collectives  70.7 us (37%)
  waiting for transfers between devices  60.9 us (32%)
  matrix products  23.2 us (12%)
  between operations  13.8 us (7%)
  other arithmetic  9.48 us (5%)
  local copies, waits for them, and re-layouts  9.04 us (5%)
    reduce_scatter x1, waiting for transfers between devices, body(): lax.psum_scatter(term, 'wide', scatter_dimension=1, tiled=True)  47.3 us
    all_gather x2, blocking collectives, apply_operator(): piece = lax.all_gather(field, 'wide', axis=1, tiled=True)  43 us
    all_gather x1, blocking collectives, body(): columns = lax.all_gather(surf_points, 'wide', axis=1, tiled=True)  23.4 us
    dot_general x8, matrix products, surface_block(): part = jnp.dot(vol_adjoint, values, preferred_element_type=jnp.float32)  14.9 us
    reduce_scatter x2, waiting for transfers between devices, apply_operator(): lax.psum_scatter(partial_rows, 'narrow', scatter_dimension=1, tiled=True)  13.5 us
    dot_general x16, matrix products, one_block(): jnp.dot(block_vals, values, precision=lax.Precision.HIGHEST, preferred_el...  8.26 us
    convert_element_type x8, other arithmetic, surface_block(): expanded = expanded.reshape(volume_rows, width).astype(jnp.float32)  6.62 us
    broadcast_in_dim x8, local copies, waits for them, and re-layouts, surface_block(): jnp.broadcast_to(mask_cols[:, None, :, None], (volume_rows // TILE, TILE,...  4.85 us
  transfers between devices with their start and end apart: 3, of which 3 were waited for; matrix products, arithmetic and copies ran while one was open for 0% of the time, Pallas kernels for 0%

commit v1 on v0

v1 whole, which is shorter than its diff:
```python
import functools
import math

import jax
import jax.numpy as jnp
from jax import lax
from jax.experimental import pallas as pl
from jax.experimental.pallas import tpu as pltpu
from jax.sharding import PartitionSpec as P

TILE = 128
CHUNK = 256
RADIUS = 0.15
KERNEL_GAIN = 3200.0
RHS_GAIN = 28.0
LOWER_EDGE = 1.0
UPPER_EDGE = 4.0
SCALE = 4.0 / RADIUS
COORD_ROWS = 56
F32 = jnp.float32
BF16 = jnp.bfloat16
MESH = pl.DeviceIdType.MESH


def split3(x):
    high = x.astype(BF16).astype(F32)
    rest = x - high
    mid = rest.astype(BF16).astype(F32)
    return high, mid, rest - mid


def features(coords, left):
    row = lax.broadcasted_iota(jnp.int32, coords.shape, 0)
    p = jnp.where(row < 3, (coords - 0.5) * SCALE, 0.0)
    norm = jnp.sum(p * p, axis=0, keepdims=True)
    nh, nm, nl = split3(jnp.broadcast_to(norm, coords.shape))
    h, m, l = split3(p)
    one = jnp.where(row < 6, 1.0, 0.0)
    if left:
        h, m, l = -2.0 * h, -2.0 * m, -2.0 * l
        last = jnp.where(row == 3, nh, jnp.where(row == 4, nm, jnp.where(row == 5, nl, one)))
        groups = [h, h, m, m, h, l, last]
    else:
        last = jnp.where(row == 0, nh, jnp.where(row == 1, nm, jnp.where(row == 2, nl, one)))
        groups = [h, m, h, m, l, h, last]
    return jnp.concatenate(groups, axis=0)


def wendland(u):
    u = jnp.maximum(u, 1e-20)
    t = u * lax.rsqrt(u)
    r = jnp.maximum(4.0 - t, 0.0)
    r2 = r * r
    return r2 * r2 * (t + 1.0)


def kernel(dims, vol_ref, adj_ref, surf_ref, mask_ref, sol_ref, res_ref,
           own_xyz, xyz_z, xyz_r, vol_own, vol_in, mask_own, mask_in, vfeat, adjs,
           sfeat, rfeat, p_hi, p_lo, piece, rhs_in, field, field_in, part, part_in,
           sem_xs, sem_xz, sem_xr, sem_v, sem_ps, sem_pr, sem_fs, sem_fr, sem_ms, sem_mr):
    N, Z, Y, C, KP = dims
    R = N * Y * C
    ADJ, NVD = adj_ref.shape
    VT, ST = mask_ref.shape
    w = lax.axis_index("wide")
    n = lax.axis_index("narrow")
    z, y, c = w // (Y * C), (w // C) % Y, w % C
    me_r = (n * Y + y) * C + c
    me_z = z * Y + y

    def r_peer(d):
        pn = lax.rem(n + d // (Y * C), N)
        py = lax.rem(y + (d // C) % Y, Y)
        pc = lax.rem(c + d % C, C)
        return {"wide": (z * Y + py) * C + pc, "narrow": pn}, (pn * Y + py) * C + pc

    def z_peer(dz, dy):
        pz = lax.rem(z + dz, Z)
        py = lax.rem(y + dy, Y)
        return {"wide": (pz * Y + py) * C + c, "narrow": n}, pz, py

    def remote(src, dst, ssem, rsem, dev):
        return pltpu.make_async_remote_copy(
            src_ref=src, dst_ref=dst, send_sem=ssem, recv_sem=rsem,
            device_id=dev, device_id_type=MESH)

    zpairs = [(dz, dy) for dz in range(Z - 1, 0, -1) for dy in range(Y)]

    barrier = pltpu.get_barrier_semaphore()
    for d in range(1, R):
        pl.semaphore_signal(barrier, inc=1, device_id=r_peer(d)[0], device_id_type=MESH)
    for dz, dy in zpairs:
        pl.semaphore_signal(barrier, inc=1, device_id=z_peer(dz, dy)[0], device_id_type=MESH)

    own_xyz[...] = jnp.zeros_like(own_xyz)
    own_xyz[0:3, :] = surf_ref[...]
    vol_own[0:ADJ, :] = adj_ref[...].astype(F32)
    vol_own[ADJ:ADJ + 8, :] = jnp.zeros((8, NVD), F32)
    vol_own[ADJ:ADJ + 3, :] = vol_ref[...]
    mask_own[...] = jnp.zeros_like(mask_own)
    mask_own[:, 0:ST] = mask_ref[...].astype(F32)
    pl.semaphore_wait(barrier, R - 1 + len(zpairs))

    sends = []
    for k, (dz, dy) in enumerate(zpairs):
        dev, pz, py = z_peer(dz, dy)
        cp = remote(own_xyz, xyz_z.at[me_z], sem_xs.at[R + k], sem_xz.at[me_z], dev)
        cp.start()
        sends.append(cp)
    for d in range(1, R):
        dev, _ = r_peer(d)
        cp = remote(own_xyz, xyz_r.at[me_r], sem_xs.at[d], sem_xr.at[me_r], dev)
        cp.start()
        sends.append(cp)
    vsends = []
    if C > 1:
        dev, _ = r_peer(1)
        for k, (src, dst) in enumerate(((vol_own, vol_in), (mask_own, mask_in))):
            cp = remote(src, dst, sem_v.at[2 * k], sem_v.at[2 * k + 1], dev)
            cp.start()
            vsends.append(cp)

    expand = (lax.broadcasted_iota(jnp.int32, (VT, NVD), 1) // TILE
              == lax.broadcasted_iota(jnp.int32, (VT, NVD), 0)).astype(F32)

    def volume_features(s, vol, mask):
        adjs[s] = vol[0:ADJ, :].astype(BF16)
        f = features(vol[ADJ:ADJ + 8, :], False)
        m = lax.dot_general(mask[...], expand, (((0,), (0,)), ((), ())),
                            preferred_element_type=F32)
        pen = (1.0 - m) * 1024.0
        vfeat[s] = jnp.concatenate([f, pen[0:KP - COORD_ROWS, :]], axis=0).astype(BF16)

    volume_features(0, vol_own, mask_own)

    xyz_r[me_r] = own_xyz[...]
    for d in range(1, R):
        dev, s = r_peer(d)
        remote(own_xyz, xyz_r.at[s], sem_xs.at[d], sem_xr.at[s], dev).wait_recv()
    for dy in range(Y):
        py = lax.rem(y + dy, Y)
        xyz_z[z * Y + py] = xyz_r[(n * Y + py) * C + c]
    for k, (dz, dy) in enumerate(zpairs):
        dev, pz, py = z_peer(dz, dy)
        s = pz * Y + py
        remote(own_xyz, xyz_z.at[s], sem_xs.at[R + k], sem_xz.at[s], dev).wait_recv()

    extra = lax.broadcasted_iota(jnp.int32, (KP - COORD_ROWS, TILE), 0)
    for s in range(Z * Y):
        hot = jnp.where(extra == s * C + c, 1.0, 0.0)
        f = jnp.concatenate([features(xyz_z[s], True), hot], axis=0)
        sfeat[s] = f.T.astype(BF16)
    if C > 1:
        for cp in vsends:
            cp.wait_recv()
        volume_features(1, vol_in, mask_in)

    def surface_block(pz):
        left = sfeat[pl.ds(pz * Y, Y)].reshape(Y * TILE, KP)
        total = jnp.zeros((ADJ, Y * TILE), F32)
        for s in range(C):
            for k in range(0, NVD, CHUNK):
                u = jnp.dot(left, vfeat[s, :, k:k + CHUNK], preferred_element_type=F32)
                total = total + lax.dot_general(
                    adjs[s, :, k:k + CHUNK], wendland(u).astype(BF16),
                    (((1,), (1,)), ((), ())), preferred_element_type=F32)
        for q in range(Y):
            piece[pz * Y + q] = total[:, q * TILE:(q + 1) * TILE]

    def piece_copy(dz, dy):
        dev, pz, py = z_peer(dz, dy)
        s = pz * Y + py
        return remote(piece.at[s], rhs_in.at[me_z], sem_ps.at[s], sem_pr.at[me_z], dev)

    def piece_arrival(dz, dy):
        dev, pz, py = z_peer(dz, dy)
        s = pz * Y + py
        return remote(piece.at[s], rhs_in.at[s], sem_ps.at[s], sem_pr.at[s], dev), s

    def far(i, carry):
        dz = Z - 1 - i
        surface_block(lax.rem(z + dz, Z))
        for dy in range(Y):
            piece_copy(dz, dy).start()
        return carry

    lax.fori_loop(0, Z - 1, far, 0)
    surface_block(z)
    for dy in range(1, Y):
        piece_copy(0, dy).start()

    for s in range(R):
        f = jnp.concatenate(
            [features(xyz_r[s], False), jnp.zeros((KP - COORD_ROWS, TILE), F32)], axis=0)
        rfeat[:, s * TILE:(s + 1) * TILE] = f.astype(BF16)

    def kernel_rows(q, carry):
        left = sfeat[q * Y + y]
        for k in range(0, R * TILE, CHUNK):
            val = wendland(jnp.dot(left, rfeat[:, k:k + CHUNK], preferred_element_type=F32))
            high = val.astype(BF16)
            p_hi[q, :, k:k + CHUNK] = high
            p_lo[q, :, k:k + CHUNK] = (val - high.astype(F32)).astype(BF16)
        return carry

    lax.fori_loop(0, Z, kernel_rows, 0)

    rhs = piece[me_z]
    order = [(0, dy) for dy in range(1, Y)] + zpairs
    for dz, dy in order:
        cp, s = piece_arrival(dz, dy)
        cp.wait_recv()
        rhs = rhs + rhs_in[s]

    total_volume = NVD * Z * Y * C
    total_surface = TILE * Z * Y * C * N
    rhs = rhs * (RHS_GAIN / math.sqrt(total_volume) / 256.0)

    def apply_operator(o, value):
        field[o] = value
        out = []
        for dz in range(1, Z):
            dev, pz, _ = z_peer(dz, 0)
            cp = remote(field.at[o], field_in.at[o, z], sem_fs.at[o, dz], sem_fr.at[o, z], dev)
            cp.start()
            out.append(cp)

        def product(f, q):
            high = f.astype(BF16)
            low = (f - high.astype(F32)).astype(BF16)
            both = jnp.dot(jnp.concatenate([high, low], axis=0), p_hi[q],
                           preferred_element_type=F32)
            return (both[0:ADJ] + both[ADJ:]
                    + jnp.dot(high, p_lo[q], preferred_element_type=F32))

        total = product(value, z)
        for dz in range(1, Z):
            dev, pz, _ = z_peer(dz, 0)
            remote(field.at[o], field_in.at[o, pz], sem_fs.at[o, dz], sem_fr.at[o, pz],
                   dev).wait_recv()
            total = total + product(field_in[o, pz], pz)
        for s in range(R):
            part[o, s] = total[:, s * TILE:(s + 1) * TILE]
        for d in range(R - 1, 0, -1):
            dev, s = r_peer(d)
            cp = remote(part.at[o, s], part_in.at[o, me_r], sem_ms.at[o, d], sem_mr.at[o, me_r],
                        dev)
            cp.start()
            out.append(cp)
        mixed = part[o, me_r]
        for d in range(1, R):
            dev, s = r_peer(d)
            remote(part.at[o, s], part_in.at[o, s], sem_ms.at[o, d], sem_mr.at[o, s],
                   dev).wait_recv()
            mixed = mixed + part_in[o, s]
        return value + (KERNEL_GAIN / total_surface / 256.0) * mixed, out

    centre = (LOWER_EDGE + UPPER_EDGE) / 2.0
    half_width = (UPPER_EDGE - LOWER_EDGE) / 2.0
    sigma = centre / half_width
    rho_zero = 1.0 / sigma
    rho_one = 1.0 / (2.0 * sigma - rho_zero)
    first = rhs / centre
    mixed, out = apply_operator(0, first)
    sends += out
    near = rhs - mixed
    update = rho_one * rho_zero * first + (2.0 * rho_one / half_width) * near
    sol_ref[...] = first + update
    mixed, out = apply_operator(1, update)
    sends += out
    res_ref[...] = near - mixed

    for cp in sends + vsends:
        cp.wait_send()
    for dz, dy in order:
        piece_copy(dz, dy).wait_send()


def body(dims, vol_points, vol_adjoint, surf_points, tile_mask):
    N, Z, Y, C, KP = dims
    R = N * Y * C
    adj, nvd = vol_adjoint.shape
    vt = tile_mask.shape[0]
    vmem = pl.BlockSpec(memory_space=pltpu.VMEM)
    out = jax.ShapeDtypeStruct((adj, TILE), F32)
    lanes = -(-tile_mask.shape[1] // 128) * 128
    dma = pltpu.SemaphoreType.DMA
    return pl.pallas_call(
        functools.partial(kernel, dims),
        out_shape=(out, out),
        in_specs=[vmem] * 4,
        out_specs=(vmem, vmem),
        scratch_shapes=[
            pltpu.VMEM((8, TILE), F32),
            pltpu.VMEM((Z * Y, 8, TILE), F32),
            pltpu.VMEM((R, 8, TILE), F32),
            pltpu.VMEM((adj + 8, nvd), F32),
            pltpu.VMEM((adj + 8, nvd), F32),
            pltpu.VMEM((vt, lanes), F32),
            pltpu.VMEM((vt, lanes), F32),
            pltpu.VMEM((C, KP, nvd), BF16),
            pltpu.VMEM((C, adj, nvd), BF16),
            pltpu.VMEM((Z * Y, TILE, KP), BF16),
            pltpu.VMEM((KP, R * TILE), BF16),
            pltpu.VMEM((Z, TILE, R * TILE), BF16),
            pltpu.VMEM((Z, TILE, R * TILE), BF16),
            pltpu.VMEM((Z * Y, adj, TILE), F32),
            pltpu.VMEM((Z * Y, adj, TILE), F32),
            pltpu.VMEM((2, adj, TILE), F32),
            pltpu.VMEM((2, Z, adj, TILE), F32),
            pltpu.VMEM((2, R, adj, TILE), F32),
            pltpu.VMEM((2, R, adj, TILE), F32),
            dma((R + Z * Y,)),
            dma((Z * Y,)),
            dma((R,)),
            dma((4,)),
            dma((Z * Y,)),
            dma((Z * Y,)),
            dma((2, Z)),
            dma((2, Z)),
            dma((2, R)),
            dma((2, R)),
        ],
        compiler_params=pltpu.CompilerParams(
            collective_id=0, has_side_effects=True, vmem_limit_bytes=56 * 1024 * 1024),
    )(vol_points, vol_adjoint, surf_points, tile_mask)


def solution(mesh):
    wide, narrow = mesh.shape["wide"], mesh.shape["narrow"]
    core = math.gcd(wide, 2)
    rows = math.gcd(wide // core, 2)
    depth = -(-(COORD_ROWS + wide) // 128) * 128
    dims = (narrow, wide // core // rows, rows, core, depth)
    return jax.shard_map(
        functools.partial(body, dims),
        mesh=mesh,
        in_specs=(
            P(None, "wide"),
            P(None, "wide"),
            P(None, ("narrow", "wide")),
            P("wide", "narrow"),
        ),
        out_specs=(P(None, ("narrow", "wide")), P(None, ("narrow", "wide"))),
        check_vma=False,
    )
```

time: 189 us -> 42 us (0.22)
  blocking collectives: 70.7 us -> 0 us
  waiting for transfers between devices: 60.9 us -> 0 us
  Pallas kernels: 0 us -> 39.2 us
  matrix products: 23.2 us -> 0 us
  between operations: 13.8 us -> 0.65 us
  other arithmetic: 9.48 us -> 0 us
  local copies, waits for them, and re-layouts: 9.04 us -> 1.96 us
    all_gather x4 -> x0, blocking collectives: 70.7 us -> none  [the longest x2 43 us: apply_operator(): piece = lax.all_gather(field, 'wide', axis=1, tiled=True)]
    reduce_scatter x3 -> x0, waiting for transfers between devices: 60.8 us -> none  [the longest x1 47.3 us: body(): lax.psum_scatter(term, 'wide', scatter_dimension=1, tiled=True)]
    pallas_call x0 -> x1, Pallas kernels: none -> 39.2 us  [body(): pl.pallas_call(functools.partial(kernel, dims), out_shape=(out, out), in_...]
    dot_general x24 -> x0, matrix products: 23.2 us -> none  [the longest x8 14.9 us: surface_block(): part = jnp.dot(vol_adjoint, values, preferred_element_type=jnp.float32)]
    convert_element_type x8 -> x0, other arithmetic: 6.62 us -> none  [surface_block(): expanded = expanded.reshape(volume_rows, width).astype(jnp.float32)]
    broadcast_in_dim x9 -> x0, local copies, waits for them, and re-layouts: 4.88 us -> none  [the longest x8 4.85 us: surface_block(): jnp.broadcast_to(mask_cols[:, None, :, None], (volume_rows // TILE, TILE,...]
    slice x32 -> x0, local copies, waits for them, and re-layouts: 2.1 us -> none  [kernel_block(): offset = sources[component][:, None] - targets[component][None, :]]
  transfers between devices with their start and end apart: 3 -> 0, of which waited for: 3 -> 0; matrix products, arithmetic and copies ran while one was open for 0% -> 0% of each run, Pallas kernels for 0% -> 0%
where the time goes in v1:
time: 42 us; the launch traced here: 41.8 us
  Pallas kernels  39.2 us (93%)
  local copies, waits for them, and re-layouts  1.96 us (5%)
  between operations  0.65 us (2%)
    pallas_call x1, Pallas kernels, body(): pl.pallas_call(functools.partial(kernel, dims), out_shape=(out, out), in_...  39.2 us
    unnamed x4, local copies, waits for them, and re-layouts  1.96 us

profile of v1, /device:TPU:0, one launch (start us, length us, event | category | flops | bytes accessed | tf_op | source)
XLA Modules:
  0.0 41.8 jit_solution(5886053369979830779)
XLA Ops:
  0.6 39.2 %shard_map.59 = (f32[48,128]{1,0:T(8,128)}, f32[48,128]{1,0:T(8,128)}) custom-call(f32[3,2048]{1,0:T(4,128)} %vol_ref.1, bf16[48,2048]{1,0:T(8,128)(2,1)} %adj_ref.1, f32[3,128]{1,0:T(4,128)} %surf_ref.1, s32[16,16]{1,0:T(8,128)} %mask_ref.1), custom_call_target="tpu_custom_call" | custom-call | tf_op jit(solution)/shard_map/pallas_call | solution.py:288
  39.8 0.0 copy-start
  39.8 1.4 %copy.8 = f32[48,128]{1,0:T(8,128)} copy(f32[48,128]{1,0:T(8,128)} %get-tuple-element.4) | data formatting | bytes 49152
  41.2 0.0 copy-done
  41.2 0.6 %copy.9 = f32[48,128]{1,0:T(8,128)} copy(f32[48,128]{1,0:T(8,128)S(1)} %copy-done) | data formatting | bytes 49152
Async XLA Ops:
  39.8 1.4 %copy-start = (f32[48,128]{1,0:T(8,128)S(1)}, f32[48,128]{1,0:T(8,128)}, u32[]{:S(2)}) copy-start(f32[48,128]{1,0:T(8,128)} %get-tuple-element.5) | copy-start | bytes 73732

commit v2 on v1

--- a/solution.py
+++ b/solution.py
@@ -54,7 +54,8 @@
     return r2 * r2 * (t + 1.0)
 
 
-def kernel(dims, vol_ref, adj_ref, surf_ref, mask_ref, sol_ref, res_ref,
+def kernel(dims, vol_hbm, adj_hbm, surf_hbm, mask_hbm, both_ref,
+           vol_ref, adj_ref, surf_ref, mask_ref, sem_in,
            own_xyz, xyz_z, xyz_r, vol_own, vol_in, mask_own, mask_in, vfeat, adjs,
            sfeat, rfeat, p_hi, p_lo, piece, rhs_in, field, field_in, part, part_in,
            sem_xs, sem_xz, sem_xr, sem_v, sem_ps, sem_pr, sem_fs, sem_fr, sem_ms, sem_mr):
@@ -86,12 +87,19 @@
 
     zpairs = [(dz, dy) for dz in range(Z - 1, 0, -1) for dy in range(Y)]
 
+    loads = [pltpu.make_async_copy(src, dst, sem_in.at[k]) for k, (src, dst) in enumerate(
+        ((surf_hbm, surf_ref), (mask_hbm, mask_ref), (vol_hbm, vol_ref), (adj_hbm, adj_ref)))]
+    for cp in loads:
+        cp.start()
+
     barrier = pltpu.get_barrier_semaphore()
     for d in range(1, R):
         pl.semaphore_signal(barrier, inc=1, device_id=r_peer(d)[0], device_id_type=MESH)
     for dz, dy in zpairs:
         pl.semaphore_signal(barrier, inc=1, device_id=z_peer(dz, dy)[0], device_id_type=MESH)
 
+    for cp in loads:
+        cp.wait()
     own_xyz[...] = jnp.zeros_like(own_xyz)
     own_xyz[0:3, :] = surf_ref[...]
     vol_own[0:ADJ, :] = adj_ref[...].astype(F32)
@@ -265,10 +273,10 @@
     sends += out
     near = rhs - mixed
     update = rho_one * rho_zero * first + (2.0 * rho_one / half_width) * near
-    sol_ref[...] = first + update
+    both_ref[0] = first + update
     mixed, out = apply_operator(1, update)
     sends += out
-    res_ref[...] = near - mixed
+    both_ref[1] = near - mixed
 
     for cp in sends + vsends:
         cp.wait_send()
@@ -282,15 +290,20 @@
     adj, nvd = vol_adjoint.shape
     vt = tile_mask.shape[0]
     vmem = pl.BlockSpec(memory_space=pltpu.VMEM)
-    out = jax.ShapeDtypeStruct((adj, TILE), F32)
+    out = jax.ShapeDtypeStruct((2, adj, TILE), F32)
     lanes = -(-tile_mask.shape[1] // 128) * 128
     dma = pltpu.SemaphoreType.DMA
-    return pl.pallas_call(
+    both = pl.pallas_call(
         functools.partial(kernel, dims),
-        out_shape=(out, out),
-        in_specs=[vmem] * 4,
-        out_specs=(vmem, vmem),
+        out_shape=out,
+        in_specs=[pl.BlockSpec(memory_space=pl.ANY)] * 4,
+        out_specs=vmem,
         scratch_shapes=[
+            pltpu.VMEM(vol_points.shape, F32),
+            pltpu.VMEM(vol_adjoint.shape, BF16),
+            pltpu.VMEM(surf_points.shape, F32),
+            pltpu.VMEM(tile_mask.shape, jnp.int32),
+            dma((4,)),
             pltpu.VMEM((8, TILE), F32),
             pltpu.VMEM((Z * Y, 8, TILE), F32),
             pltpu.VMEM((R, 8, TILE), F32),
@@ -324,6 +337,7 @@
         compiler_params=pltpu.CompilerParams(
             collective_id=0, has_side_effects=True, vmem_limit_bytes=56 * 1024 * 1024),
     )(vol_points, vol_adjoint, surf_points, tile_mask)
+    return both[0], both[1]
 
 
 def solution(mesh):

time: 42 us -> 40.6 us (0.967)
  Pallas kernels: 39.2 us -> 38.4 us
  local copies, waits for them, and re-layouts: 1.96 us -> 1.38 us
    unnamed x4 -> x0, local copies, waits for them, and re-layouts: 1.96 us -> none
    squeeze x0 -> x1, local copies, waits for them, and re-layouts: none -> 1.38 us  [body(): return (both[0], both[1])]
    pallas_call x1, Pallas kernels: 39.2 us -> 38.4 us  [body(): pl.pallas_call(functools.partial(kernel, dims), out_shape=out, in_specs=[...]
where the time goes in v2:
time: 40.6 us; the launch traced here: 40.4 us
  Pallas kernels  38.4 us (95%)
  local copies, waits for them, and re-layouts  1.38 us (3%)
  between operations  0.64 us (2%)
    pallas_call x1, Pallas kernels, body(): pl.pallas_call(functools.partial(kernel, dims), out_shape=out, in_specs=[...  38.4 us
    squeeze x1, local copies, waits for them, and re-layouts, body(): return (both[0], both[1])  1.38 us

profile of v2, /device:TPU:0, one launch (start us, length us, event | category | flops | bytes accessed | tf_op | source)
XLA Modules:
  0.0 40.4 jit_solution(1588581795326881914)
XLA Ops:
  0.6 38.4 %shard_map.59 = f32[2,48,128]{2,1,0:T(8,128)} custom-call(f32[3,2048]{1,0:T(4,128)} %vol_hbm.1, bf16[48,2048]{1,0:T(8,128)(2,1)} %adj_hbm.1, f32[3,128]{1,0:T(4,128)} %surf_hbm.1, s32[16,16]{1,0:T(8,128)} %mask_hbm.1), custom_call_target="tpu_custom_call" | custom-call | tf_op jit(solution)/shard_map/pallas_call | solution.py:296
  39.0 1.4 %slice_bitcast_fusion = (f32[48,128]{1,0:T(8,128)}, f32[48,128]{1,0:T(8,128)}) fusion(f32[2,48,128]{2,1,0:T(8,128)} %shard_map.59), kind=kLoop, calls=%fused_computation | loop fusion | bytes 98304 | tf_op jit(solution)/shard_map/squeeze | solution.py:340

commit v3 on v2

--- a/solution.py
+++ b/solution.py
@@ -129,15 +129,16 @@
             vsends.append(cp)
 
     expand = (lax.broadcasted_iota(jnp.int32, (VT, NVD), 1) // TILE
-              == lax.broadcasted_iota(jnp.int32, (VT, NVD), 0)).astype(F32)
+              == lax.broadcasted_iota(jnp.int32, (VT, NVD), 0)).astype(F32).astype(BF16)
+    listed = -(-ST // 8) * 8
 
     def volume_features(s, vol, mask):
         adjs[s] = vol[0:ADJ, :].astype(BF16)
         f = features(vol[ADJ:ADJ + 8, :], False)
-        m = lax.dot_general(mask[...], expand, (((0,), (0,)), ((), ())),
-                            preferred_element_type=F32)
-        pen = (1.0 - m) * 1024.0
-        vfeat[s] = jnp.concatenate([f, pen[0:KP - COORD_ROWS, :]], axis=0).astype(BF16)
+        off = ((1.0 - mask[...]) * 1024.0).T[0:listed].astype(BF16)
+        pen = jnp.dot(off, expand, preferred_element_type=F32)
+        rest = jnp.zeros((KP - COORD_ROWS - listed, NVD), F32)
+        vfeat[s] = jnp.concatenate([f, pen, rest], axis=0).astype(BF16)
 
     volume_features(0, vol_own, mask_own)
 
@@ -227,7 +228,7 @@
     def apply_operator(o, value):
         field[o] = value
         out = []
-        for dz in range(1, Z):
+        for dz in range(Z - 1, 0, -1):
             dev, pz, _ = z_peer(dz, 0)
             cp = remote(field.at[o], field_in.at[o, z], sem_fs.at[o, dz], sem_fr.at[o, z], dev)
             cp.start()

time: 40.6 us -> 40.7 us (level)
  no operation moved by 1% of the time
where the time goes in v3:
time: 40.7 us; the launch traced here: 40.5 us
  Pallas kernels  38.5 us (95%)
  local copies, waits for them, and re-layouts  1.38 us (3%)
  between operations  0.64 us (2%)
    pallas_call x1, Pallas kernels, body(): pl.pallas_call(functools.partial(kernel, dims), out_shape=out, in_specs=[...  38.5 us
    squeeze x1, local copies, waits for them, and re-layouts, body(): return (both[0], both[1])  1.38 us

profile of v3, /device:TPU:0, one launch (start us, length us, event | category | flops | bytes accessed | tf_op | source)
XLA Modules:
  0.0 40.5 jit_solution(17108122613248983393)
XLA Ops:
  0.6 38.5 %shard_map.59 = f32[2,48,128]{2,1,0:T(8,128)} custom-call(f32[3,2048]{1,0:T(4,128)} %vol_hbm.1, bf16[48,2048]{1,0:T(8,128)(2,1)} %adj_hbm.1, f32[3,128]{1,0:T(4,128)} %surf_hbm.1, s32[16,16]{1,0:T(8,128)} %mask_hbm.1), custom_call_target="tpu_custom_call" | custom-call | tf_op jit(solution)/shard_map/pallas_call | solution.py:297
  39.1 1.4 %slice_bitcast_fusion = (f32[48,128]{1,0:T(8,128)}, f32[48,128]{1,0:T(8,128)}) fusion(f32[2,48,128]{2,1,0:T(8,128)} %shard_map.59), kind=kLoop, calls=%fused_computation | loop fusion | bytes 98304 | tf_op jit(solution)/shard_map/squeeze | solution.py:341
